TPU v7x, 128 devices: a whole 4x4x4 slice. The times are simulated.
128 devices in a mesh: dp: 64 (over z_hi, x, y, core), tensor: 2 (over z_lo).
Axes of the slice: x: 4, y: 4, z: 4 (z_hi: 2, z_lo: 2; z = z_hi * 2 + z_lo), core: 2. Of those that a mesh axis runs over, the one named last changes fastest.
Arguments:
- layer_input: bfloat16 [32768, 768], P('dp'), may hold values from -6 to 6
- seg_ids: int32 [32768], P('dp'), may hold values from 0 to 127, never falling along the last dimension, each value on 1 to 2048 neighbouring positions
- ln1_gain: float32 [768], replicated, may hold values from 0.5 to 1.5
- ln1_bias: float32 [768], replicated, may hold values from -2.5 to 2.5
- ln2_gain: float32 [768], replicated, may hold values from 0.5 to 1.5
- ln2_bias: float32 [768], replicated, may hold values from -2.5 to 2.5
- w_qkv: bfloat16 [768, 12, 192], P(None, 'tensor'), may hold values from -0.21875 to 0.21875
- b_qkv: float32 [12, 192], P('tensor'), may hold values from -2.5 to 2.5
- w_out: bfloat16 [12, 64, 768], P('tensor'), may hold values from -0.625 to 0.625
- b_out: float32 [768], replicated, may hold values from -2.5 to 2.5
- w_fc: bfloat16 [768, 3072], P(None, 'tensor'), may hold values from -0.21875 to 0.21875
- b_fc: float32 [3072], P('tensor'), may hold values from -2.5 to 2.5
- w_proj: bfloat16 [3072, 768], P('tensor'), may hold values from -0.109375 to 0.109375
- b_proj: float32 [768], replicated, may hold values from -2.5 to 2.5
- cotangent: float32 [32768, 768], P('dp'), may hold values from -6 to 6
Outputs:
- layer_output: bfloat16 [32768, 768], P('dp')
- grad_input: float32 [32768, 768], P('dp')
- grad_ln1_gain: float32 [768], replicated
- grad_ln1_bias: float32 [768], replicated
- grad_ln2_gain: float32 [768], replicated
- grad_ln2_bias: float32 [768], replicated
- grad_w_qkv: float32 [768, 12, 192], P(None, 'tensor')
- grad_b_qkv: float32 [12, 192], P('tensor')
- grad_w_out: float32 [12, 64, 768], P('tensor')
- grad_b_out: float32 [768], replicated
- grad_w_fc: float32 [768, 3072], P(None, 'tensor')
- grad_b_fc: float32 [3072], P('tensor')
- grad_w_proj: float32 [3072, 768], P('tensor')
- grad_b_proj: float32 [768], replicated
Inputs may be any that keep to these rules, and one draw needn't show every extreme that they name: `seg_ids`: document numbers never fall from one token to the next.
All inputs are finite; a program needn't handle non-finite values.
Results may differ from a plain program's by a relative error of at most 0.0098.
Values may be sent and summed in bfloat16 or wider, within the bound.
No kernel may reach another device: no remote copies, remote signals or barrier semaphores. Data moves between devices by JAX's collectives and lax.ppermute only.
A program may use at most 128 MiB of HBM per device.

v0:
```python
import jax
import jax.numpy as jnp
from jax import lax
from jax.sharding import PartitionSpec as P

HD = 64
ROT = 16
SEQ = 512
epsilon = 1e-05
masked_score = -1000000000.0


def norm_rows(row_values, gain_vec, shift_vec):
    row_mean = jnp.mean(row_values, axis=-1, keepdims=True)
    centred = row_values - row_mean
    variance = jnp.mean(centred * centred, axis=-1, keepdims=True)
    return centred * lax.rsqrt(variance + epsilon) * gain_vec + shift_vec


def rotate(row_values, cosine_table, sine_table):
    half_rot = ROT // 2
    leading = row_values[..., :half_rot]
    trailing = row_values[..., half_rot:ROT]
    cosine_col = cosine_table[:, None, :]
    sine_col = sine_table[:, None, :]
    return jnp.concatenate(
        [
            leading * cosine_col - trailing * sine_col,
            trailing * cosine_col + leading * sine_col,
            row_values[..., ROT:],
        ],
        axis=-1,
    )


def tables(segments):
    indices = jnp.arange(SEQ, dtype=jnp.int32)
    starts = jnp.concatenate([jnp.ones((1,), dtype=bool), segments[1:] != segments[:-1]])
    opening = lax.cummax(jnp.where(starts, indices, 0), axis=0)
    offset = (indices - opening).astype(jnp.float32)
    frequency = 10000.0 ** (jnp.arange(ROT // 2).astype(jnp.float32) * (-2.0 / ROT))
    angles = offset[:, None] * frequency[None, :]
    allowed = (segments[:, None] == segments[None, :]) & (indices[:, None] >= indices[None, :])
    return (jnp.cos(angles), jnp.sin(angles), allowed)


def gelu_exact(row_values):
    return jax.nn.gelu(row_values, approximate=False)


def contract_rows(left_mat, right_mat):
    return lax.dot_general(
        left_mat, right_mat, (((0,), (0,)), ((), ())), preferred_element_type=jnp.float32
    )


def contract_cols(left_mat, right_mat):
    return lax.dot_general(
        left_mat, right_mat, (((1,), (1,)), ((), ())), preferred_element_type=jnp.float32
    )


def body(
    layer_input,
    seg_ids,
    ln1_gain,
    ln1_bias,
    ln2_gain,
    ln2_bias,
    w_qkv,
    b_qkv,
    w_out,
    b_out,
    w_fc,
    b_fc,
    w_proj,
    b_proj,
    cotangent,
):
    tok_rows = layer_input.shape[0]
    model_width = layer_input.shape[1]
    head_count = w_qkv.shape[1]
    seq_count = tok_rows // SEQ
    score_scale = HD ** (-0.5)
    x_float = layer_input.astype(jnp.float32)
    normed_attn, pull_attn = jax.vjp(norm_rows, x_float, ln1_gain, ln1_bias)
    normed_mlp, pull_mlp = jax.vjp(norm_rows, x_float, ln2_gain, ln2_bias)
    attn_in = normed_attn.astype(jnp.bfloat16)
    mlp_in = normed_mlp.astype(jnp.bfloat16)
    flat_qkv = w_qkv.reshape(model_width, head_count * 3 * HD)
    mixed_qkv = (
        jnp.dot(attn_in, flat_qkv, preferred_element_type=jnp.float32).reshape(
            tok_rows, head_count, 3 * HD
        )
        + b_qkv
    )
    hidden = jnp.dot(mlp_in, w_fc, preferred_element_type=jnp.float32) + b_fc
    activated, pull_gelu = jax.vjp(gelu_exact, hidden)
    act_low = activated.astype(jnp.bfloat16)
    seg_blocks = seg_ids.reshape(seq_count, SEQ)

    def attend_forward(packed):
        mixed_seq, segments = packed
        cosine_table, sine_table, allowed = tables(segments)
        queries = rotate(mixed_seq[..., :HD], cosine_table, sine_table).astype(jnp.bfloat16)
        keys_rot = rotate(mixed_seq[..., HD : 2 * HD], cosine_table, sine_table).astype(
            jnp.bfloat16
        )
        values = mixed_seq[..., 2 * HD :].astype(jnp.bfloat16)
        scores = (
            jnp.einsum("qhd,khd->hqk", queries, keys_rot, preferred_element_type=jnp.float32)
            * score_scale
        )
        scores = jnp.where(allowed[None], scores, masked_score)
        row_top = jnp.max(scores, axis=-1, keepdims=True)
        powers = jnp.exp(scores - row_top)
        totals = jnp.sum(powers, axis=-1, keepdims=True)
        weights = (powers / totals).astype(jnp.bfloat16)
        context = jnp.einsum("hqk,khd->qhd", weights, values, preferred_element_type=jnp.float32)
        return (context.astype(jnp.bfloat16), row_top + jnp.log(totals), queries, keys_rot, values)

    context, log_totals, queries_all, keys_all, values_all = lax.map(
        attend_forward, (mixed_qkv.reshape(seq_count, SEQ, head_count, 3 * HD), seg_blocks)
    )
    context_flat = context.reshape(tok_rows, head_count * HD)
    flat_out = w_out.reshape(head_count * HD, model_width)
    partial_value = jnp.dot(context_flat, flat_out, preferred_element_type=jnp.float32) + jnp.dot(
        act_low, w_proj, preferred_element_type=jnp.float32
    )
    output = (
        x_float
        + lax.psum(partial_value.astype(jnp.bfloat16), "tensor").astype(jnp.float32)
        + b_out
        + b_proj
    ).astype(jnp.bfloat16)
    grad_low = cotangent.astype(jnp.bfloat16)
    grad_shift = jnp.sum(cotangent, axis=0)
    grad_w_proj = contract_rows(act_low, grad_low)
    grad_act = contract_cols(grad_low, w_proj)
    grad_hidden = pull_gelu(grad_act)[0].astype(jnp.bfloat16)
    grad_b_fc = jnp.sum(grad_hidden, axis=0, dtype=jnp.float32)
    grad_w_fc = contract_rows(mlp_in, grad_hidden)
    grad_mlp_in = contract_cols(grad_hidden, w_fc)
    grad_w_out = contract_rows(context_flat, grad_low).reshape(w_out.shape)
    grad_context = (
        contract_cols(grad_low, flat_out)
        .astype(jnp.bfloat16)
        .reshape(seq_count, SEQ, head_count, HD)
    )

    def attend_backward(packed):
        queries, keys_rot, values, log_seq, grad_seq, segments = packed
        cosine_table, sine_table, allowed = tables(segments)
        scores = (
            jnp.einsum("qhd,khd->hqk", queries, keys_rot, preferred_element_type=jnp.float32)
            * score_scale
        )
        scores = jnp.where(allowed[None], scores, masked_score)
        probabilities = jnp.exp(scores - log_seq)
        grad_values = jnp.einsum(
            "hqk,qhd->khd",
            probabilities.astype(jnp.bfloat16),
            grad_seq,
            preferred_element_type=jnp.float32,
        )
        grad_probs = jnp.einsum(
            "qhd,khd->hqk", grad_seq, values, preferred_element_type=jnp.float32
        )
        grad_scores = (
            probabilities
            * (grad_probs - jnp.sum(probabilities * grad_probs, axis=-1, keepdims=True))
        ).astype(jnp.bfloat16)
        grad_queries = (
            jnp.einsum("hqk,khd->qhd", grad_scores, keys_rot, preferred_element_type=jnp.float32)
            * score_scale
        )
        grad_keys = (
            jnp.einsum("hqk,qhd->khd", grad_scores, queries, preferred_element_type=jnp.float32)
            * score_scale
        )
        return jnp.concatenate(
            [
                rotate(grad_queries, cosine_table, -sine_table),
                rotate(grad_keys, cosine_table, -sine_table),
                grad_values,
            ],
            axis=-1,
        )

    grad_mixed = lax.map(
        attend_backward, (queries_all, keys_all, values_all, log_totals, grad_context, seg_blocks)
    )
    grad_mixed = grad_mixed.reshape(tok_rows, head_count * 3 * HD).astype(jnp.bfloat16)
    grad_b_qkv = jnp.sum(grad_mixed, axis=0, dtype=jnp.float32).reshape(head_count, 3 * HD)
    grad_w_qkv = contract_rows(attn_in, grad_mixed).reshape(w_qkv.shape)
    grad_attn_in = contract_cols(grad_mixed, flat_qkv)
    grad_x_attn, grad_gain_attn, grad_bias_attn = pull_attn(grad_attn_in)
    grad_x_mlp, grad_gain_mlp, grad_bias_mlp = pull_mlp(grad_mlp_in)
    summed_x, gain_attn, bias_attn, gain_mlp, bias_mlp = (
        lax.psum((grad_x_attn + grad_x_mlp).astype(jnp.bfloat16), "tensor").astype(jnp.float32),
        lax.psum(grad_gain_attn.astype(jnp.bfloat16), "tensor").astype(jnp.float32),
        lax.psum(grad_bias_attn.astype(jnp.bfloat16), "tensor").astype(jnp.float32),
        lax.psum(grad_gain_mlp.astype(jnp.bfloat16), "tensor").astype(jnp.float32),
        lax.psum(grad_bias_mlp.astype(jnp.bfloat16), "tensor").astype(jnp.float32),
    )
    grad_x = cotangent + summed_x
    shares = (
        lax.psum_scatter(grad_w_qkv, "dp", scatter_dimension=0, tiled=True),
        lax.psum_scatter(grad_b_qkv, "dp", scatter_dimension=1, tiled=True),
        lax.psum_scatter(grad_w_out, "dp", scatter_dimension=2, tiled=True),
        lax.psum_scatter(grad_w_fc, "dp", scatter_dimension=0, tiled=True),
        lax.psum_scatter(grad_b_fc, "dp", scatter_dimension=0, tiled=True),
        lax.psum_scatter(grad_w_proj, "dp", scatter_dimension=1, tiled=True),
        lax.psum_scatter(grad_shift, "dp", scatter_dimension=0, tiled=True),
        lax.psum_scatter(gain_attn, "dp", scatter_dimension=0, tiled=True),
        lax.psum_scatter(bias_attn, "dp", scatter_dimension=0, tiled=True),
        lax.psum_scatter(gain_mlp, "dp", scatter_dimension=0, tiled=True),
        lax.psum_scatter(bias_mlp, "dp", scatter_dimension=0, tiled=True),
    )
    whole_grads = (
        lax.all_gather(shares[0].astype(jnp.bfloat16), "dp", axis=0, tiled=True).astype(
            jnp.float32
        ),
        lax.all_gather(shares[1].astype(jnp.bfloat16), "dp", axis=1, tiled=True).astype(
            jnp.float32
        ),
        lax.all_gather(shares[2].astype(jnp.bfloat16), "dp", axis=2, tiled=True).astype(
            jnp.float32
        ),
        lax.all_gather(shares[3].astype(jnp.bfloat16), "dp", axis=0, tiled=True).astype(
            jnp.float32
        ),
        lax.all_gather(shares[4].astype(jnp.bfloat16), "dp", axis=0, tiled=True).astype(
            jnp.float32
        ),
        lax.all_gather(shares[5].astype(jnp.bfloat16), "dp", axis=1, tiled=True).astype(
            jnp.float32
        ),
        lax.all_gather(shares[6].astype(jnp.bfloat16), "dp", axis=0, tiled=True).astype(
            jnp.float32
        ),
        lax.all_gather(shares[7].astype(jnp.bfloat16), "dp", axis=0, tiled=True).astype(
            jnp.float32
        ),
        lax.all_gather(shares[8].astype(jnp.bfloat16), "dp", axis=0, tiled=True).astype(
            jnp.float32
        ),
        lax.all_gather(shares[9].astype(jnp.bfloat16), "dp", axis=0, tiled=True).astype(
            jnp.float32
        ),
        lax.all_gather(shares[10].astype(jnp.bfloat16), "dp", axis=0, tiled=True).astype(
            jnp.float32
        ),
    )
    return (
        output,
        grad_x,
        whole_grads[7],
        whole_grads[8],
        whole_grads[9],
        whole_grads[10],
        whole_grads[0],
        whole_grads[1],
        whole_grads[2],
        whole_grads[6],
        whole_grads[3],
        whole_grads[4],
        whole_grads[5],
        whole_grads[6],
    )


def solution(mesh):
    placed = (
        P("dp", None),
        P("dp"),
        P(),
        P(),
        P(),
        P(),
        P(None, "tensor", None),
        P("tensor", None),
        P("tensor", None, None),
        P(),
        P(None, "tensor"),
        P("tensor"),
        P("tensor", None),
        P(),
        P("dp", None),
    )
    return jax.shard_map(
        body,
        mesh=mesh,
        in_specs=placed,
        out_specs=(
            P("dp", None),
            P("dp", None),
            P(),
            P(),
            P(),
            P(),
            P(None, "tensor", None),
            P("tensor", None),
            P("tensor", None, None),
            P(),
            P(None, "tensor"),
            P("tensor"),
            P("tensor", None),
            P(),
        ),
        check_vma=False,
    )
```

profile of v0, /device:TPU:1, one launch (start us, length us, event | category | flops | bytes accessed | tf_op | source)
XLA Modules:
  0.0 1356.6 jit_solution(9484674918558623280)
XLA Ops:
  9.0 1.7 fusion.53
  13.5 4.4 fusion.88
  20.9 2.2 fusion.89
  24.4 2.0 fusion.50
  28.0 1.9 multiply_reduce_fusion
  29.9 2.6 multiply_convert_fusion
  37.0 9.2 convert_reduce_fusion
  53.4 1.7 bitcast_reduce_fusion
  56.6 1.8 add_convert_fusion.1
  58.5 5.3 fusion.51
  64.2 3.5 fusion.55
  69.0 5.3 all-reduce.21
  74.3 370.4 %all-reduce.28 = (bf16[768]{0:T(1024)(128)(2,1)}, bf16[768]{0:T(1024)(128)(2,1)}, bf16[768]{0:T(1024)(128)(2,1)}, bf16[768]{0:T(1024)(128)(2,1)}, bf16[768,6,192...) all-reduce(bf16[768]{0:T(1024)(128)(2,1)S(1)} %get-tuple-element.14, ...), channel_id=2, replica_groups=mesh['dp'=64,'tensor'=2] {'dp'}, use_global_device_ids=true, to_apply=%region_15.16.clone | all-reduce | flops 1186176 | bytes 7110912
  446.3 5.3 fusion.75
  451.7 3.6 fusion.92
  455.3 196.0 %fusion.81 = (f32[16,1536]{1,0:T(8,128)S(1)}, f32[1536,16]{0,1:T(8,128)S(1)}) fusion(f32[768,1536]{1,0:T(8,128)} %fusion.75, f32[1536,768]{0,1:T(8,128)} %fusion.92), kind=kCustom, calls=%all-reduce-scatter.2 | all-reduce-scatter fusion | flops 3145729 | bytes 9634304
  652.7 8.6 collective-permute-start.30
  666.5 6.8 collective-permute-start.25
  674.7 1.6 collective-permute-start.23
  676.3 3.1 collective-permute-start.22
  679.5 3.5 collective-permute-start.21
  683.0 2.5 collective-permute-start.20
  685.5 3.9 collective-permute-start.19
  689.4 3.6 collective-permute-start.18
  693.0 2.2 collective-permute-start.17
  695.2 1.9 collective-permute-start.16
  698.4 24.8 %concatenate.28 = bf16[1536,268]{0,1:T(8,128)(2,1)} concatenate(bf16[1536,12]{0,1:T(8,128)(2,1)S(1)} %collective-permute-done.31, bf16[1536,16]{0,1:T(8,128)(2,1)S(1)} %collective-permute-done.30, bf16[1536,16]{0,1:T(8,128)(2,1)S(1)} %collective-permute-done.29, bf16[1536,16]{0,1:T(8,128)(2,1)} %copy-done.23, bf16[1536,16]{0,1:T(8,128)(2,1)} %copy-done.24, ...), dimensions={1} | concatenate | bytes 1695744
  724.9 3.0 collective-permute-start.15
  727.9 4.9 collective-permute-start.14
  736.7 4.8 collective-permute-start.10
  742.9 3.3 collective-permute-start.8
  746.2 1.6 collective-permute-start.7
  749.1 4.2 collective-permute-start.5
  753.4 2.8 collective-permute-start.4
  756.2 4.1 collective-permute-start.3
  760.3 2.7 collective-permute-start.2
  763.1 2.5 collective-permute-start.1
  765.6 2.2 collective-permute-start
  769.1 24.7 %concatenate.27 = bf16[268,1536]{1,0:T(8,128)(2,1)} concatenate(bf16[12,1536]{1,0:T(8,128)(2,1)S(1)} %collective-permute-done.15, bf16[16,1536]{1,0:T(8,128)(2,1)S(1)} %collective-permute-done.14, bf16[16,1536]{1,0:T(8,128)(2,1)S(1)} %collective-permute-done.13, bf16[16,1536]{1,0:T(8,128)(2,1)S(1)} %collective-permute-done.12, bf16[16,1536]{1,0:T(8,128)(2,1)S(1)} %collective-permute-done.11, ...), dimensions={0} | concatenate | bytes 1695744
  801.8 316.2 %all-reduce.20 = (bf16[768]{0:T(1024)(128)(2,1)S(1)}, bf16[768]{0:T(1024)(128)(2,1)S(1)}, bf16[768]{0:T(1024)(128)(2,1)S(1)}, bf16[768]{0:T(1024)(128)(2,1)S(1)}...) all-reduce(bf16[768]{0:T(1024)(128)(2,1)S(1)} %dynamic-update-slice, ...), channel_id=1, replica_groups=mesh['dp'=64,'tensor'=2] {'dp'}, use_global_device_ids=true, to_apply=%add | all-reduce | flops 5376 | bytes 21504
  1121.7 96.1 %all-gather = bf16[64,3,6]{2,1,0:T(4,128)(2,1)S(1)} all-gather(bf16[1,3,6]{2,1,0:T(4,128)(2,1)S(1)} %fusion.68), channel_id=1, replica_groups=mesh['dp'=64,'tensor'=2] {'dp'}, dimensions={0}, use_global_device_ids=true | all-gather | bytes 2340 | tf_op jit(solution)/shard_map/all_gather | solution.py:224
  1219.6 99.8 %all_gather.39 = bf16[6,64,768]{1,0,2:T(8,128)(2,1)} all-gather(bf16[6,64,12]{1,0,2:T(8,128)(2,1)S(1)} %copy.72), channel_id=1, replica_groups=mesh['dp'=64,'tensor'=2] {'dp'}, dimensions={2}, use_global_device_ids=true | all-gather | bytes 599040 | tf_op jit(solution)/shard_map/all_gather | solution.py:227
  1319.4 2.8 copy.74
  1322.8 2.4 fusion.40
  1326.6 5.1 copy.73
  1331.7 5.2 reshape.320
  1336.9 6.0 copy.75
  1343.0 5.2 reshape.306
  (252 shorter events, 56.2 us)
Async XLA Ops:
  8.0 29.0 %copy-start = (bf16[1536,768]{1,0:T(8,128)(2,1)S(1)}, bf16[1536,768]{1,0:T(8,128)(2,1)}, u32[]{:S(2)}) copy-start(bf16[1536,768]{1,0:T(8,128)(2,1)} %param.27) | copy-start | bytes 7077892
  8.0 1314.8 %all-reduce.27.cloned.1.call-start = ((), (), s32[]{:S(2)}) async-start(), calls=%async_computation.3 | async-start | bytes 3145728 | tf_op jit(solution)/shard_map/psum | solution.py:132
  58.5 1268.1 %all-gather.7.cloned.1.call-start = ((), (), s32[]{:S(2)}) async-start(), calls=%async_computation | async-start | bytes 3194880 | tf_op jit(solution)/shard_map/all_gather | solution.py:221
  74.2 372.1 %copy-start.46 = (f32[768]{0:T(1024)S(1)}, f32[768]{0:T(1024)}, u32[]{:S(2)}) copy-start(f32[768]{0:T(1024)} %param.19) | copy-start | bytes 9220
  74.2 372.1 %copy-start.57 = (f32[768]{0:T(1024)S(1)}, f32[768]{0:T(1024)}, u32[]{:S(2)}) copy-start(f32[768]{0:T(1024)} %param.20) | copy-start | bytes 9220
  446.3 885.5 %all-gather.11.cloned.1.call-start = ((), (), s32[]{:S(2)}) async-start(), calls=%async_computation.2 | async-start | bytes 3194880 | tf_op jit(solution)/shard_map/all_gather | solution.py:236
  651.4 13.8 %collective-permute-start.31 = (bf16[1536,12]{0,1:T(8,128)(2,1)S(1)}, bf16[1536,12]{0,1:T(8,128)(2,1)S(1)}, u32[]{:S(2)}, u32[]{:S(2)}) collective-permute-start(bf16[1536,12]{0,1:T(8,128)(2,1)S(1)} %slice.115), channel_id=1, source_target_pairs={{0,32},{2,34},{4,36},{6,38},{8,40},{10,42},{12,44},{14,46},{16,48}... | collective-permute-start | bytes 110600
  652.7 13.8 %collective-permute-start.30 = (bf16[1536,16]{0,1:T(8,128)(2,1)S(1)}, bf16[1536,16]{0,1:T(8,128)(2,1)S(1)}, u32[]{:S(2)}, u32[]{:S(2)}) collective-permute-start(bf16[1536,16]{0,1:T(8,128)(2,1)S(1)} %convert.90), channel_id=1, source_target_pairs={{0,30},{2,32},{4,34},{6,36},{8,38},{10,40},{12,42},{14,44},{16,46}... | collective-permute-start | bytes 147464
  661.3 12.1 collective-permute-start.29
  662.6 12.1 collective-permute-start.28
  663.9 12.4 collective-permute-start.27
  665.2 14.3 %collective-permute-start.26 = (bf16[1536,16]{0,1:T(8,128)(2,1)S(1)}, bf16[1536,16]{0,1:T(8,128)(2,1)S(1)}, u32[]{:S(2)}, u32[]{:S(2)}) collective-permute-start(bf16[1536,16]{0,1:T(8,128)(2,1)S(1)} %convert.90), channel_id=1, source_target_pairs={{0,22},{2,24},{4,26},{6,28},{8,30},{10,32},{12,34},{14,36},{16,38}... | collective-permute-start | bytes 147464
  666.5 16.5 %collective-permute-start.25 = (bf16[1536,16]{0,1:T(8,128)(2,1)S(1)}, bf16[1536,16]{0,1:T(8,128)(2,1)S(1)}, u32[]{:S(2)}, u32[]{:S(2)}) collective-permute-start(bf16[1536,16]{0,1:T(8,128)(2,1)S(1)} %convert.90), channel_id=1, source_target_pairs={{0,20},{2,22},{4,24},{6,26},{8,28},{10,30},{12,32},{14,34},{16,36}... | collective-permute-start | bytes 147464
  673.4 12.1 collective-permute-start.24
  674.7 22.4 %copy-start.23 = (bf16[1536,16]{0,1:T(8,128)(2,1)}, bf16[1536,16]{0,1:T(8,128)(2,1)S(1)}, u32[]{:S(2)}) copy-start(bf16[1536,16]{0,1:T(8,128)(2,1)S(1)} %collective-permute-done.28) | copy-start | bytes 147460
  674.7 14.7 %collective-permute-start.23 = (bf16[1536,16]{0,1:T(8,128)(2,1)S(1)}, bf16[1536,16]{0,1:T(8,128)(2,1)S(1)}, u32[]{:S(2)}, u32[]{:S(2)}) collective-permute-start(bf16[1536,16]{0,1:T(8,128)(2,1)S(1)} %convert.90), channel_id=1, source_target_pairs={{0,16},{2,18},{4,20},{6,22},{8,24},{10,26},{12,28},{14,30},{16,32}... | collective-permute-start | bytes 147464
  676.3 20.8 %copy-start.24 = (bf16[1536,16]{0,1:T(8,128)(2,1)}, bf16[1536,16]{0,1:T(8,128)(2,1)S(1)}, u32[]{:S(2)}) copy-start(bf16[1536,16]{0,1:T(8,128)(2,1)S(1)} %collective-permute-done.27) | copy-start | bytes 147460
  676.3 16.6 %collective-permute-start.22 = (bf16[1536,16]{0,1:T(8,128)(2,1)S(1)}, bf16[1536,16]{0,1:T(8,128)(2,1)S(1)}, u32[]{:S(2)}, u32[]{:S(2)}) collective-permute-start(bf16[1536,16]{0,1:T(8,128)(2,1)S(1)} %convert.90), channel_id=1, source_target_pairs={{0,14},{2,16},{4,18},{6,20},{8,22},{10,24},{12,26},{14,28},{16,30}... | collective-permute-start | bytes 147464
  679.5 17.6 %copy-start.25 = (bf16[1536,16]{0,1:T(8,128)(2,1)}, bf16[1536,16]{0,1:T(8,128)(2,1)S(1)}, u32[]{:S(2)}) copy-start(bf16[1536,16]{0,1:T(8,128)(2,1)S(1)} %collective-permute-done.26) | copy-start | bytes 147460
  679.5 15.7 %collective-permute-start.21 = (bf16[1536,16]{0,1:T(8,128)(2,1)S(1)}, bf16[1536,16]{0,1:T(8,128)(2,1)S(1)}, u32[]{:S(2)}, u32[]{:S(2)}) collective-permute-start(bf16[1536,16]{0,1:T(8,128)(2,1)S(1)} %convert.90), channel_id=1, source_target_pairs={{0,12},{2,14},{4,16},{6,18},{8,20},{10,22},{12,24},{14,26},{16,28}... | collective-permute-start | bytes 147464
  683.0 14.2 %copy-start.26 = (bf16[1536,16]{0,1:T(8,128)(2,1)}, bf16[1536,16]{0,1:T(8,128)(2,1)S(1)}, u32[]{:S(2)}) copy-start(bf16[1536,16]{0,1:T(8,128)(2,1)S(1)} %collective-permute-done.25) | copy-start | bytes 147460
  683.0 14.8 %collective-permute-start.20 = (bf16[1536,16]{0,1:T(8,128)(2,1)S(1)}, bf16[1536,16]{0,1:T(8,128)(2,1)}, u32[]{:S(2)}, u32[]{:S(2)}) collective-permute-start(bf16[1536,16]{0,1:T(8,128)(2,1)S(1)} %convert.90), channel_id=1, source_target_pairs={{0,10},{2,12},{4,14},{6,16},{8,18},{10,20},{12,22},{14,24},{16,26}... | collective-permute-start | bytes 147464
  685.5 12.4 collective-permute-start.19
  689.4 8.5 collective-permute-start.18
  693.0 4.9 collective-permute-start.17
  695.2 3.2 collective-permute-start.16
  724.8 618.1 %all-gather.9.cloned.1.call-start = ((), (), s32[]{:S(2)}) async-start(), calls=%async_computation.1 | async-start | bytes 3194880 | tf_op jit(solution)/shard_map/all_gather | solution.py:230
  724.9 11.8 collective-permute-start.15
  727.9 13.7 %collective-permute-start.14 = (bf16[16,1536]{1,0:T(8,128)(2,1)S(1)}, bf16[16,1536]{1,0:T(8,128)(2,1)S(1)}, u32[]{:S(2)}, u32[]{:S(2)}) collective-permute-start(bf16[16,1536]{1,0:T(8,128)(2,1)S(1)} %convert.91), channel_id=1, source_target_pairs={{0,30},{2,32},{4,34},{6,36},{8,38},{10,40},{12,42},{14,44},{16,46}... | collective-permute-start | bytes 147464
  732.8 10.1 collective-permute-start.13
  734.1 12.0 collective-permute-start.12
  735.4 12.4 collective-permute-start.11
  736.7 12.4 collective-permute-start.10
  741.6 11.8 collective-permute-start.9
  742.9 13.3 collective-permute-start.8
  746.2 14.1 %collective-permute-start.7 = (bf16[16,1536]{1,0:T(8,128)(2,1)S(1)}, bf16[16,1536]{1,0:T(8,128)(2,1)S(1)}, u32[]{:S(2)}, u32[]{:S(2)}) collective-permute-start(bf16[16,1536]{1,0:T(8,128)(2,1)S(1)} %convert.91), channel_id=1, source_target_pairs={{0,16},{2,18},{4,20},{6,22},{8,24},{10,26},{12,28},{14,30},{16,32}... | collective-permute-start | bytes 147464
  747.8 15.2 %collective-permute-start.6 = (bf16[16,1536]{1,0:T(8,128)(2,1)S(1)}, bf16[16,1536]{1,0:T(8,128)(2,1)S(1)}, u32[]{:S(2)}, u32[]{:S(2)}) collective-permute-start(bf16[16,1536]{1,0:T(8,128)(2,1)S(1)} %convert.91), channel_id=1, source_target_pairs={{0,14},{2,16},{4,18},{6,20},{8,22},{10,24},{12,26},{14,28},{16,30}... | collective-permute-start | bytes 147464
  749.1 16.5 %collective-permute-start.5 = (bf16[16,1536]{1,0:T(8,128)(2,1)S(1)}, bf16[16,1536]{1,0:T(8,128)(2,1)S(1)}, u32[]{:S(2)}, u32[]{:S(2)}) collective-permute-start(bf16[16,1536]{1,0:T(8,128)(2,1)S(1)} %convert.91), channel_id=1, source_target_pairs={{0,12},{2,14},{4,16},{6,18},{8,20},{10,22},{12,24},{14,26},{16,28}... | collective-permute-start | bytes 147464
  753.4 14.6 %copy-start.28 = (bf16[16,1536]{1,0:T(8,128)(2,1)}, bf16[16,1536]{1,0:T(8,128)(2,1)S(1)}, u32[]{:S(2)}) copy-start(bf16[16,1536]{1,0:T(8,128)(2,1)S(1)} %collective-permute-done.9) | copy-start | bytes 147460
  753.4 14.5 %collective-permute-start.4 = (bf16[16,1536]{1,0:T(8,128)(2,1)S(1)}, bf16[16,1536]{1,0:T(8,128)(2,1)S(1)}, u32[]{:S(2)}, u32[]{:S(2)}) collective-permute-start(bf16[16,1536]{1,0:T(8,128)(2,1)S(1)} %convert.91), channel_id=1, source_target_pairs={{0,10},{2,12},{4,14},{6,16},{8,18},{10,20},{12,22},{14,24},{16,26}... | collective-permute-start | bytes 147464
  756.2 11.7 copy-start.30
  756.2 11.7 collective-permute-start.3
  760.3 7.6 collective-permute-start.2
  763.1 4.8 collective-permute-start.1
  765.6 3.5 collective-permute-start
  1218.0 104.8 %copy-start.48 = (f32[768]{0:T(1024)S(1)}, f32[768]{0:T(1024)}, u32[]{:S(2)}) copy-start(f32[768]{0:T(1024)} %param.28) | copy-start | bytes 9220
  1218.0 104.8 %copy-start.49 = (f32[768]{0:T(1024)S(1)}, f32[768]{0:T(1024)}, u32[]{:S(2)}) copy-start(f32[768]{0:T(1024)} %param.24) | copy-start | bytes 9220
  1322.2 25.9 %copy-start.43 = (f32[768]{0:T(1024)}, f32[768]{0:T(1024)S(1)}, u32[]{:S(2)}) copy-start(f32[768]{0:T(1024)S(1)} %convert_element_type.231) | copy-start | bytes 9220
  (47 other events, 139.3 us)
Sparse Core Ops, SparseCore 0:
  58.6 67.3 all-reduce.26
Sparse Core Ops, SparseCore 1:
  446.3 79.1 all-gather.6
  724.9 69.2 all-gather.10
  797.7 67.3 all-gather.8
where the time goes:
time: 1370 us; the launch traced here: 1360 us
  blocking collectives  1080 us (79%)
  local copies, waits for them, and re-layouts  92 us (7%)
  starting transfers between devices  88.3 us (6%)
  matrix products  48.2 us (4%)
  other arithmetic  22.5 us (2%)
  between operations  21 us (2%)
    unnamed x3, blocking collectives  883 us
    all_gather x1, blocking collectives, body(): lax.all_gather(shares[2].astype(jnp.bfloat16), 'dp', axis=2, tiled=True)  99.8 us
    all_gather x1, blocking collectives, body(): lax.all_gather(shares[1].astype(jnp.bfloat16), 'dp', axis=1, tiled=True)  96.1 us
    unnamed x32, starting transfers between devices  88.1 us
    unnamed x150, local copies, waits for them, and re-layouts  78 us
  transfers between devices with their start and end apart: 36, of which 1 were waited for; matrix products, arithmetic and copies ran while one was open for 22% of the time, Pallas kernels for 0%

commit v1 on v0

--- a/solution.py
+++ b/solution.py
@@ -224,9 +224,12 @@
         lax.all_gather(shares[1].astype(jnp.bfloat16), "dp", axis=1, tiled=True).astype(
             jnp.float32
         ),
-        lax.all_gather(shares[2].astype(jnp.bfloat16), "dp", axis=2, tiled=True).astype(
-            jnp.float32
-        ),
+        jnp.concatenate(
+            lax.all_to_all(
+                jnp.stack([shares[2].astype(jnp.bfloat16)] * lax.axis_size("dp")), "dp", 0, 0
+            ),
+            axis=2,
+        ).astype(jnp.float32),
         lax.all_gather(shares[3].astype(jnp.bfloat16), "dp", axis=0, tiled=True).astype(
             jnp.float32
         ),

time: 1370 us -> 1240 us (0.905)
  blocking collectives: 1080 us -> 991 us
  local copies, waits for them, and re-layouts: 92 us -> 47.6 us
    all_gather x1 -> x0, blocking collectives: 99.8 us -> none  [body(): lax.all_gather(shares[2].astype(jnp.bfloat16), 'dp', axis=2, tiled=True)]
    unnamed x150 -> x121, local copies, waits for them, and re-layouts: 78 us -> 28.9 us
  transfers between devices with their start and end apart: 36 -> 37, of which waited for: 1 -> 2; matrix products, arithmetic and copies ran while one was open for 22% -> 21% of each run, Pallas kernels for 0% -> 0%
where the time goes in v1:
time: 1240 us; the launch traced here: 1230 us
  blocking collectives  991 us (80%)
  starting transfers between devices  96 us (8%)
  local copies, waits for them, and re-layouts  47.6 us (4%)
  matrix products  46.7 us (4%)
  other arithmetic  22.8 us (2%)
  between operations  21 us (2%)
    unnamed x3, blocking collectives  889 us
    all_gather x1, blocking collectives, body(): lax.all_gather(shares[1].astype(jnp.bfloat16), 'dp', axis=1, tiled=True)  96.1 us
    unnamed x32, starting transfers between devices  88.5 us
    unnamed x121, local copies, waits for them, and re-layouts  28.9 us
  transfers between devices with their start and end apart: 37, of which 2 were waited for; matrix products, arithmetic and copies ran while one was open for 21% of the time, Pallas kernels for 0%

profile of v1, /device:TPU:1, one launch (start us, length us, event | category | flops | bytes accessed | tf_op | source)
XLA Modules:
  0.0 1226.4 jit_solution(12714244955889635307)
XLA Ops:
  9.0 1.7 fusion.53
  13.5 4.4 fusion.88
  20.9 2.2 fusion.89
  24.4 2.0 fusion.50
  28.0 1.9 multiply_reduce_fusion
  29.9 2.6 multiply_convert_fusion
  37.0 9.2 convert_reduce_fusion
  53.4 1.7 bitcast_reduce_fusion
  56.5 1.8 add_convert_fusion.1
  58.4 5.3 fusion.51
  64.1 2.1 fusion.55
  67.5 4.9 all-reduce.21
  72.4 370.6 %all-reduce.28 = (bf16[768]{0:T(1024)(128)(2,1)S(1)}, bf16[768]{0:T(1024)(128)(2,1)S(1)}, bf16[768]{0:T(1024)(128)(2,1)S(1)}, bf16[768]{0:T(1024)(128)(2,1)S(1)}...) all-reduce(bf16[768]{0:T(1024)(128)(2,1)S(1)} %get-tuple-element.14, ...), channel_id=2, replica_groups=mesh['dp'=64,'tensor'=2] {'dp'}, use_global_device_ids=true, to_apply=%region_15.16.clone | all-reduce | flops 1186176 | bytes 7110912
  444.7 5.3 fusion.75
  450.0 3.6 fusion.92
  453.6 195.9 %fusion.81 = (f32[16,1536]{1,0:T(8,128)S(1)}, f32[1536,16]{0,1:T(8,128)S(1)}) fusion(f32[768,1536]{1,0:T(8,128)} %fusion.75, f32[1536,768]{0,1:T(8,128)} %fusion.92), kind=kCustom, calls=%all-reduce-scatter.2 | all-reduce-scatter fusion | flops 3145729 | bytes 9634304
  650.9 9.0 collective-permute-start.30
  665.2 6.8 collective-permute-start.25
  674.9 3.1 collective-permute-start.22
  678.1 3.5 collective-permute-start.21
  681.6 1.9 collective-permute-start.20
  683.4 3.9 collective-permute-start.19
  687.3 3.3 collective-permute-start.18
  690.6 2.5 collective-permute-start.17
  693.1 2.1 collective-permute-start.16
  696.4 2.6 concatenate.28
  699.7 3.5 collective-permute-start.15
  703.3 4.8 collective-permute-start.14
  712.0 5.0 collective-permute-start.10
  718.3 3.1 collective-permute-start.8
  724.4 4.2 collective-permute-start.5
  728.7 2.8 collective-permute-start.4
  731.5 4.0 collective-permute-start.3
  735.5 2.8 collective-permute-start.2
  738.3 2.5 collective-permute-start.1
  740.9 2.2 collective-permute-start
  744.2 2.6 concatenate.27
  750.0 7.4 all-to-all-start
  761.1 323.0 %all-reduce.20 = (bf16[768]{0:T(1024)(128)(2,1)S(1)}, bf16[768]{0:T(1024)(128)(2,1)S(1)}, bf16[768]{0:T(1024)(128)(2,1)S(1)}, bf16[768]{0:T(1024)(128)(2,1)S(1)}...) all-reduce(bf16[768]{0:T(1024)(128)(2,1)S(1)} %dynamic-update-slice, ...), channel_id=1, replica_groups=mesh['dp'=64,'tensor'=2] {'dp'}, use_global_device_ids=true, to_apply=%add | all-reduce | flops 5376 | bytes 21504
  1087.1 96.1 %all-gather = bf16[64,3,6]{2,1,0:T(4,128)(2,1)S(1)} all-gather(bf16[1,3,6]{2,1,0:T(4,128)(2,1)S(1)} %fusion.68), channel_id=1, replica_groups=mesh['dp'=64,'tensor'=2] {'dp'}, dimensions={0}, use_global_device_ids=true | all-gather | bytes 2340 | tf_op jit(solution)/shard_map/all_gather | solution.py:224
  1186.1 2.0 copy.72
  1188.1 2.6 reshape.288
  1190.8 1.7 copy.74
  1192.5 2.4 fusion.40
  1196.3 5.1 copy.73
  1201.4 5.2 reshape.327
  1206.6 6.2 copy.75
  1212.8 5.2 reshape.313
  (226 shorter events, 57.1 us)
Async XLA Ops:
  8.0 29.0 %copy-start = (bf16[1536,768]{1,0:T(8,128)(2,1)S(1)}, bf16[1536,768]{1,0:T(8,128)(2,1)}, u32[]{:S(2)}) copy-start(bf16[1536,768]{1,0:T(8,128)(2,1)} %param.27) | copy-start | bytes 7077892
  8.0 1184.5 %all-reduce.27.cloned.1.call-start = ((), (), s32[]{:S(2)}) async-start(), calls=%async_computation.4 | async-start | bytes 3145728 | tf_op jit(solution)/shard_map/psum | solution.py:132
  13.5 4.4 copy-start.24
  18.9 4.2 copy-start.12
  58.3 1137.9 %all-gather.7.cloned.1.call-start = ((), (), s32[]{:S(2)}) async-start(), calls=%async_computation.1 | async-start | bytes 3194880 | tf_op jit(solution)/shard_map/all_gather | solution.py:221
  58.4 5.3 copy-start.11
  63.7 8.7 copy-start.26
  72.4 372.3 %copy-start.30 = (f32[768]{0:T(1024)S(1)}, f32[768]{0:T(1024)}, u32[]{:S(2)}) copy-start(f32[768]{0:T(1024)} %param.19) | copy-start | bytes 9220
  72.4 372.3 %copy-start.41 = (f32[768]{0:T(1024)S(1)}, f32[768]{0:T(1024)}, u32[]{:S(2)}) copy-start(f32[768]{0:T(1024)} %param.20) | copy-start | bytes 9220
  444.6 5.4 copy-start.4
  444.6 5.4 copy-start.7
  444.6 756.8 %all-gather.11.cloned.1.call-start = ((), (), s32[]{:S(2)}) async-start(), calls=%async_computation.3 | async-start | bytes 3194880 | tf_op jit(solution)/shard_map/all_gather | solution.py:239
  649.6 14.3 %collective-permute-start.31 = (bf16[1536,12]{0,1:T(8,128)(2,1)S(1)}, bf16[1536,12]{0,1:T(8,128)(2,1)S(1)}, u32[]{:S(2)}, u32[]{:S(2)}) collective-permute-start(bf16[1536,12]{0,1:T(8,128)(2,1)S(1)} %slice.115), channel_id=1, source_target_pairs={{0,32},{2,34},{4,36},{6,38},{8,40},{10,42},{12,44},{14,46},{16,48}... | collective-permute-start | bytes 110600
  650.9 14.3 %collective-permute-start.30 = (bf16[1536,16]{0,1:T(8,128)(2,1)S(1)}, bf16[1536,16]{0,1:T(8,128)(2,1)S(1)}, u32[]{:S(2)}, u32[]{:S(2)}) collective-permute-start(bf16[1536,16]{0,1:T(8,128)(2,1)S(1)} %convert.92), channel_id=1, source_target_pairs={{0,30},{2,32},{4,34},{6,36},{8,38},{10,40},{12,42},{14,44},{16,46}... | collective-permute-start | bytes 147464
  659.9 12.1 collective-permute-start.29
  661.2 12.1 collective-permute-start.28
  662.5 12.4 %collective-permute-start.27 = (bf16[1536,16]{0,1:T(8,128)(2,1)S(1)}, bf16[1536,16]{0,1:T(8,128)(2,1)S(1)}, u32[]{:S(2)}, u32[]{:S(2)}) collective-permute-start(bf16[1536,16]{0,1:T(8,128)(2,1)S(1)} %convert.92), channel_id=1, source_target_pairs={{0,24},{2,26},{4,28},{6,30},{8,32},{10,34},{12,36},{14,38},{16,40}... | collective-permute-start | bytes 147464
  663.8 14.2 %collective-permute-start.26 = (bf16[1536,16]{0,1:T(8,128)(2,1)S(1)}, bf16[1536,16]{0,1:T(8,128)(2,1)S(1)}, u32[]{:S(2)}, u32[]{:S(2)}) collective-permute-start(bf16[1536,16]{0,1:T(8,128)(2,1)S(1)} %convert.92), channel_id=1, source_target_pairs={{0,22},{2,24},{4,26},{6,28},{8,30},{10,32},{12,34},{14,36},{16,38}... | collective-permute-start | bytes 147464
  665.2 16.4 %collective-permute-start.25 = (bf16[1536,16]{0,1:T(8,128)(2,1)S(1)}, bf16[1536,16]{0,1:T(8,128)(2,1)S(1)}, u32[]{:S(2)}, u32[]{:S(2)}) collective-permute-start(bf16[1536,16]{0,1:T(8,128)(2,1)S(1)} %convert.92), channel_id=1, source_target_pairs={{0,20},{2,22},{4,24},{6,26},{8,28},{10,30},{12,32},{14,34},{16,36}... | collective-permute-start | bytes 147464
  672.0 11.4 collective-permute-start.24
  673.3 14.0 %collective-permute-start.23 = (bf16[1536,16]{0,1:T(8,128)(2,1)S(1)}, bf16[1536,16]{0,1:T(8,128)(2,1)S(1)}, u32[]{:S(2)}, u32[]{:S(2)}) collective-permute-start(bf16[1536,16]{0,1:T(8,128)(2,1)S(1)} %convert.92), channel_id=1, source_target_pairs={{0,16},{2,18},{4,20},{6,22},{8,24},{10,26},{12,28},{14,30},{16,32}... | collective-permute-start | bytes 147464
  674.9 15.7 %collective-permute-start.22 = (bf16[1536,16]{0,1:T(8,128)(2,1)S(1)}, bf16[1536,16]{0,1:T(8,128)(2,1)S(1)}, u32[]{:S(2)}, u32[]{:S(2)}) collective-permute-start(bf16[1536,16]{0,1:T(8,128)(2,1)S(1)} %convert.92), channel_id=1, source_target_pairs={{0,14},{2,16},{4,18},{6,20},{8,22},{10,24},{12,26},{14,28},{16,30}... | collective-permute-start | bytes 147464
  678.1 15.0 %collective-permute-start.21 = (bf16[1536,16]{0,1:T(8,128)(2,1)S(1)}, bf16[1536,16]{0,1:T(8,128)(2,1)S(1)}, u32[]{:S(2)}, u32[]{:S(2)}) collective-permute-start(bf16[1536,16]{0,1:T(8,128)(2,1)S(1)} %convert.92), channel_id=1, source_target_pairs={{0,12},{2,14},{4,16},{6,18},{8,20},{10,22},{12,24},{14,26},{16,28}... | collective-permute-start | bytes 147464
  681.6 14.3 %collective-permute-start.20 = (bf16[1536,16]{0,1:T(8,128)(2,1)S(1)}, bf16[1536,16]{0,1:T(8,128)(2,1)S(1)}, u32[]{:S(2)}, u32[]{:S(2)}) collective-permute-start(bf16[1536,16]{0,1:T(8,128)(2,1)S(1)} %convert.92), channel_id=1, source_target_pairs={{0,10},{2,12},{4,14},{6,16},{8,18},{10,20},{12,22},{14,24},{16,26}... | collective-permute-start | bytes 147464
  683.4 12.5 %collective-permute-start.19 = (bf16[1536,16]{0,1:T(8,128)(2,1)S(1)}, bf16[1536,16]{0,1:T(8,128)(2,1)S(1)}, u32[]{:S(2)}, u32[]{:S(2)}) collective-permute-start(bf16[1536,16]{0,1:T(8,128)(2,1)S(1)} %convert.92), channel_id=1, source_target_pairs={{0,8},{2,10},{4,12},{6,14},{8,16},{10,18},{12,20},{14,22},{16,24},... | collective-permute-start | bytes 147464
  687.3 8.6 collective-permute-start.18
  690.6 5.3 collective-permute-start.17
  693.1 3.3 collective-permute-start.16
  699.7 513.1 %all-gather.9.cloned.1.call-start = ((), (), s32[]{:S(2)}) async-start(), calls=%async_computation.2 | async-start | bytes 3194880 | tf_op jit(solution)/shard_map/all_gather | solution.py:233
  699.7 12.3 %collective-permute-start.15 = (bf16[12,1536]{1,0:T(8,128)(2,1)S(1)}, bf16[12,1536]{1,0:T(8,128)(2,1)S(1)}, u32[]{:S(2)}, u32[]{:S(2)}) collective-permute-start(bf16[12,1536]{1,0:T(8,128)(2,1)S(1)} %slice.114), channel_id=1, source_target_pairs={{0,32},{2,34},{4,36},{6,38},{8,40},{10,42},{12,44},{14,46},{16,48}... | collective-permute-start | bytes 110600
  703.3 13.7 %collective-permute-start.14 = (bf16[16,1536]{1,0:T(8,128)(2,1)S(1)}, bf16[16,1536]{1,0:T(8,128)(2,1)S(1)}, u32[]{:S(2)}, u32[]{:S(2)}) collective-permute-start(bf16[16,1536]{1,0:T(8,128)(2,1)S(1)} %convert.93), channel_id=1, source_target_pairs={{0,30},{2,32},{4,34},{6,36},{8,38},{10,40},{12,42},{14,44},{16,46}... | collective-permute-start | bytes 147464
  708.1 10.2 collective-permute-start.13
  709.4 12.0 collective-permute-start.12
  710.7 12.4 %collective-permute-start.11 = (bf16[16,1536]{1,0:T(8,128)(2,1)S(1)}, bf16[16,1536]{1,0:T(8,128)(2,1)S(1)}, u32[]{:S(2)}, u32[]{:S(2)}) collective-permute-start(bf16[16,1536]{1,0:T(8,128)(2,1)S(1)} %convert.93), channel_id=1, source_target_pairs={{0,24},{2,26},{4,28},{6,30},{8,32},{10,34},{12,36},{14,38},{16,40}... | collective-permute-start | bytes 147464
  712.0 12.4 %collective-permute-start.10 = (bf16[16,1536]{1,0:T(8,128)(2,1)S(1)}, bf16[16,1536]{1,0:T(8,128)(2,1)S(1)}, u32[]{:S(2)}, u32[]{:S(2)}) collective-permute-start(bf16[16,1536]{1,0:T(8,128)(2,1)S(1)} %convert.93), channel_id=1, source_target_pairs={{0,22},{2,24},{4,26},{6,28},{8,30},{10,32},{12,34},{14,36},{16,38}... | collective-permute-start | bytes 147464
  717.0 11.6 collective-permute-start.9
  718.3 13.2 %collective-permute-start.8 = (bf16[16,1536]{1,0:T(8,128)(2,1)S(1)}, bf16[16,1536]{1,0:T(8,128)(2,1)S(1)}, u32[]{:S(2)}, u32[]{:S(2)}) collective-permute-start(bf16[16,1536]{1,0:T(8,128)(2,1)S(1)} %convert.93), channel_id=1, source_target_pairs={{0,18},{2,20},{4,22},{6,24},{8,26},{10,28},{12,30},{14,32},{16,34}... | collective-permute-start | bytes 147464
  721.5 14.1 %collective-permute-start.7 = (bf16[16,1536]{1,0:T(8,128)(2,1)S(1)}, bf16[16,1536]{1,0:T(8,128)(2,1)S(1)}, u32[]{:S(2)}, u32[]{:S(2)}) collective-permute-start(bf16[16,1536]{1,0:T(8,128)(2,1)S(1)} %convert.93), channel_id=1, source_target_pairs={{0,16},{2,18},{4,20},{6,22},{8,24},{10,26},{12,28},{14,30},{16,32}... | collective-permute-start | bytes 147464
  723.1 15.2 %collective-permute-start.6 = (bf16[16,1536]{1,0:T(8,128)(2,1)S(1)}, bf16[16,1536]{1,0:T(8,128)(2,1)S(1)}, u32[]{:S(2)}, u32[]{:S(2)}) collective-permute-start(bf16[16,1536]{1,0:T(8,128)(2,1)S(1)} %convert.93), channel_id=1, source_target_pairs={{0,14},{2,16},{4,18},{6,20},{8,22},{10,24},{12,26},{14,28},{16,30}... | collective-permute-start | bytes 147464
  724.4 16.4 %collective-permute-start.5 = (bf16[16,1536]{1,0:T(8,128)(2,1)S(1)}, bf16[16,1536]{1,0:T(8,128)(2,1)S(1)}, u32[]{:S(2)}, u32[]{:S(2)}) collective-permute-start(bf16[16,1536]{1,0:T(8,128)(2,1)S(1)} %convert.93), channel_id=1, source_target_pairs={{0,12},{2,14},{4,16},{6,18},{8,20},{10,22},{12,24},{14,26},{16,28}... | collective-permute-start | bytes 147464
  728.7 14.4 %collective-permute-start.4 = (bf16[16,1536]{1,0:T(8,128)(2,1)S(1)}, bf16[16,1536]{1,0:T(8,128)(2,1)S(1)}, u32[]{:S(2)}, u32[]{:S(2)}) collective-permute-start(bf16[16,1536]{1,0:T(8,128)(2,1)S(1)} %convert.93), channel_id=1, source_target_pairs={{0,10},{2,12},{4,14},{6,16},{8,18},{10,20},{12,22},{14,24},{16,26}... | collective-permute-start | bytes 147464
  731.5 11.6 collective-permute-start.3
  735.5 7.6 collective-permute-start.2
  738.3 4.8 collective-permute-start.1
  740.9 3.4 collective-permute-start
  750.0 434.8 %all-to-all-start = ((bf16[64,2,2304]{2,1,0:T(2,128)(2,1)}), bf16[64,2,2304]{2,1,0:T(2,128)(2,1)S(1)}, u32[]{:S(2)}, u32[]{:S(2)}) async-start(bf16[64,2,2304]{2,1,0:T(2,128)(2,1)} %reshape.349), calls=%async_computation | async-start | bytes 1179648 | tf_op jit(solution)/shard_map/all_to_all | solution.py:228
  1184.2 33.8 %copy-start.27 = (f32[768]{0:T(1024)}, f32[768]{0:T(1024)S(1)}, u32[]{:S(2)}) copy-start(f32[768]{0:T(1024)S(1)} %convert_element_type.239) | copy-start | bytes 9220
  1206.6 12.0 copy-start.1
  (32 other events, 63.2 us)
Sparse Core Ops, SparseCore 0:
  58.5 68.0 all-reduce.26
Sparse Core Ops, SparseCore 1:
  444.7 79.4 all-gather.6
  699.8 70.7 all-gather.10
  774.1 68.5 all-gather.8
